TPU v7x, 32 devices: a whole 2x2x4 slice. The times are simulated.
32 devices in a mesh: grp: 2 (over y), db: 4 (over z), head: 2 (over x), sub: 2 (over core).
Axes of the slice: x: 2, y: 2, z: 4, core: 2. Of those that a mesh axis runs over, the one named last changes fastest.
Arguments:
- activations: bfloat16 [512, 8192], P(('grp', 'head', 'sub'), 'db'), parts along dimension 0, may hold values from -24 to 24
- w_query: bfloat16 [8192, 4096], P('db', ('head', 'sub')), may hold values from -0.0625 to 0.0625
- w_out: bfloat16 [4096, 8192], P(('head', 'sub'), 'db'), may hold values from -0.09375 to 0.09375
- w_up: bfloat16 [8192, 16384], P('db', ('head', 'sub')), may hold values from -0.0625 to 0.0625
- w_down: bfloat16 [16384, 8192], P(('head', 'sub'), 'db'), may hold values from -0.09375 to 0.09375
- kv_store: bfloat16 [64, 2, 128, 4096], P(('grp', 'db'), None, None, ('head', 'sub')), parts along dimension 0, may hold values from -330 to 330
- neighbours: int32 [8, 2], P('grp'), parts along dimension 0, may hold values from 0 to 31, as said below
- block_place: int32 [64], P('grp'), parts along dimension 0, may hold values from 0 to 31, as said below
Outputs:
- layer_out: bfloat16 [512, 8192], P(('grp', 'head', 'sub'), 'db'), parts along dimension 0
There are 2 independent parts, one for each index of `grp`. A program takes and returns all parts, laid end to end along the dimension named above; an argument that names none is the same for every part. Nothing has to cross between parts.
Inputs may be any that keep to these rules, and one draw needn't show every extreme that they name: `neighbours`: the 2 blocks named by a span and the 2 blocks named by the span before it lie on 4 different shards, the shard of block b being block_place[b] // 8. Each store position appears once; block b is kept at position block_place[b] of kv_store.
All inputs are finite; a program needn't handle non-finite values.
Results may differ from a plain program's by a relative error of at most 0.017.
Values may be sent and summed in bfloat16 or wider, within the bound.
A program may use at most 128 MiB of HBM per device.

v0:
```python
import jax
import jax.numpy as jnp
from jax import lax
from jax.sharding import PartitionSpec as P

D = 8192
HDIM = 128
NEIGH = 2
NTOK = 128


def apply_norm(values, row_sums):
    row_mean = row_sums[0] / D
    row_var = row_sums[1] / D - row_mean * row_mean
    return ((values - row_mean) * lax.rsqrt(row_var + 1e-05)).astype(jnp.bfloat16)


def local(activations, w_query, w_out, w_up, w_down, kv_store, neighbours, block_place):
    shards = lax.axis_size("db")
    my_index = lax.axis_index("db")
    inputs = lax.all_gather(activations, ("head", "sub"), axis=0, tiled=True).astype(jnp.float32)
    sums_in = lax.psum(
        (jnp.sum(inputs, axis=1, keepdims=True), jnp.sum(inputs * inputs, axis=1, keepdims=True)),
        "db",
    )
    normed = apply_norm(inputs, sums_in)
    queries = lax.psum_scatter(
        jnp.dot(normed, w_query, preferred_element_type=jnp.float32),
        "db",
        scatter_dimension=0,
        tiled=True,
    ).astype(jnp.bfloat16)
    local_width = queries.shape[1]
    head_count = local_width // HDIM
    span_rows = queries.shape[0]
    earlier = lax.dynamic_slice_in_dim(neighbours, jnp.maximum(my_index - 1, 0), 1, 0)
    current = lax.dynamic_slice_in_dim(neighbours, my_index, 1, 0)
    wanted = jnp.concatenate([earlier, current], 0).reshape(-1)
    block_ids = jnp.arange(block_place.shape[0], dtype=jnp.int32)
    located = jnp.sum(
        jnp.where(block_ids[None, :] == wanted[:, None], block_place[None, :], 0), axis=1
    )
    store_blocks = kv_store.shape[0]
    owner_of = located // store_blocks
    slot_of = located % store_blocks
    request_ids = jnp.arange(2 * NEIGH, dtype=jnp.int32)
    segment_of = (request_ids >= NEIGH).astype(jnp.int32)
    usable = jnp.where(request_ids < NEIGH, my_index > 0, True)
    peer_ids = jnp.arange(shards, dtype=jnp.int32)
    coded_slot = 2 * slot_of + segment_of + 1
    request_out = (
        jnp.sum(
            jnp.where(
                (owner_of[None, :] == peer_ids[:, None]) & usable[None, :], coded_slot[None, :], 0
            ),
            axis=1,
            keepdims=True,
        )
        - 1
    )
    request_in = lax.all_to_all(request_out, "db", split_axis=0, concat_axis=0, tiled=True)
    asked_for = request_in[:, 0]
    chosen_slot = jnp.maximum(asked_for, 0) // 2
    row_index = jnp.arange(span_rows, dtype=jnp.int32)
    row_segment = (row_index == span_rows - 1).astype(jnp.int32)
    row_live = (row_index == span_rows - 1) | (my_index > 0)
    score_scale = HDIM ** (-0.5)
    outgoing = jnp.take(kv_store, chosen_slot, axis=0)
    outgoing = jnp.where((asked_for >= 0)[:, None, None, None], outgoing, jnp.zeros_like(outgoing))
    arrived = lax.all_to_all(outgoing, "db", split_axis=0, concat_axis=0, tiled=True)
    needed = jnp.take(arrived, owner_of, axis=0)
    key_block = needed[:, 0].reshape(-1, head_count, HDIM)
    value_block = needed[:, 1].reshape(-1, head_count, HDIM)
    query_heads = queries.reshape(span_rows, head_count, HDIM)
    scores = (
        jnp.einsum("rhe,khe->hrk", query_heads, key_block, preferred_element_type=jnp.float32)
        * score_scale
    )
    key_request = jnp.arange(key_block.shape[0], dtype=jnp.int32) // NTOK
    key_live = (segment_of[key_request][None, :] == row_segment[:, None]) & usable[key_request][
        None, :
    ]
    scores = jnp.where(key_live[None], scores, -1e30)
    top_score = jnp.max(scores, axis=-1, keepdims=True)
    exponent = jnp.exp(scores - top_score)
    weights = (exponent / jnp.sum(exponent, axis=-1, keepdims=True)).astype(jnp.bfloat16)
    attended = jnp.einsum("hrk,khe->rhe", weights, value_block, preferred_element_type=jnp.float32)
    attended = attended.reshape(span_rows, local_width).astype(jnp.bfloat16)
    attended = jnp.where(row_live[:, None], attended, jnp.zeros_like(attended))
    attn_part = jnp.dot(
        lax.all_gather(attended, "db", axis=0, tiled=True),
        w_out,
        preferred_element_type=jnp.float32,
    )
    attn_full = lax.psum(attn_part, ("head", "sub"))
    state_rows = inputs + attn_full
    sums_mid = lax.psum(
        (
            jnp.sum(state_rows, axis=1, keepdims=True),
            jnp.sum(state_rows * state_rows, axis=1, keepdims=True),
        ),
        "db",
    )
    normed_mid = apply_norm(state_rows, sums_mid)
    lifted = lax.psum_scatter(
        jnp.dot(normed_mid, w_up, preferred_element_type=jnp.float32).astype(jnp.bfloat16),
        "db",
        scatter_dimension=0,
        tiled=True,
    ).astype(jnp.float32)
    activated = jax.nn.gelu(lifted, approximate=True).astype(jnp.bfloat16)
    gathered = lax.all_gather(activated, "db", axis=0, tiled=True)
    group_rows = state_rows.shape[0] // lax.axis_size(("head", "sub"))
    lowered = lax.psum_scatter(
        jnp.dot(gathered, w_down, preferred_element_type=jnp.float32).astype(jnp.bfloat16),
        ("head", "sub"),
        scatter_dimension=0,
        tiled=True,
    ).astype(jnp.float32)
    own_state = lax.dynamic_slice_in_dim(
        state_rows, lax.axis_index(("head", "sub")) * group_rows, group_rows, 0
    )
    return (own_state + lowered).astype(jnp.bfloat16)


def solution(mesh):
    in_specs = (
        P(("grp", "head", "sub"), "db"),
        P("db", ("head", "sub")),
        P(("head", "sub"), "db"),
        P("db", ("head", "sub")),
        P(("head", "sub"), "db"),
        P(("grp", "db"), None, None, ("head", "sub")),
        P("grp", None),
        P("grp"),
    )
    out_specs = P(("grp", "head", "sub"), "db")
    return jax.shard_map(local, mesh=mesh, in_specs=in_specs, out_specs=out_specs, check_vma=False)
```

profile of v0, /device:TPU:1, one launch (start us, length us, event | category | flops | bytes accessed | tf_op | source)
XLA Modules:
  0.0 342.1 jit_solution(5223061935545655713)
XLA Ops:
  6.5 0.8 constant_dynamic-slice_fusion.1
  7.4 0.1 pad_add_fusion
  7.4 0.1 copy.28
  7.5 0.1 eq.62
  7.6 0.8 select_reduce_fusion.2
  8.5 0.1 select_reduce_fusion.1
  8.6 0.7 copy.29
  9.3 5.4 %all-to-all-start = ((s32[4,1,1]{2,1,0:T(1,128)}), s32[4,1,1]{2,1,0:T(1,128)S(1)}, u32[]{:S(2)}, u32[]{:S(2)}) async-start(s32[4,1,1]{2,1,0:T(1,128)} %copy.29), calls=%async_computation | async-start | bytes 4096 | tf_op jit(solution)/shard_map/all_to_all | solution.py:61
  14.7 0.0 all-gather.3.cloned.1.call-start
  14.7 0.7 all-gather.3.cloned.1.call-update
  15.4 3.6 %all-to-all-done = s32[4,1,1]{2,1,0:T(1,128)S(1)} async-done(((s32[4,1,1]{2,1,0:T(1,128)}), s32[4,1,1]{2,1,0:T(1,128)S(1)}, u32[]{:S(2)}, u32[]{:S(2)}) %all-to-all-start) | async-done | bytes 48 | tf_op jit(solution)/shard_map/all_to_all | solution.py:61
  19.0 0.2 compare_reduce_fusion
  19.3 0.2 shift-right-logical_reduce_fusion
  19.5 2.9 gather_fusion
  22.4 1.6 select_select_fusion
  24.0 3.6 %all-to-all-start.1 = ((bf16[4,2,128,1024]{3,2,1,0:T(8,128)(2,1)}), bf16[4,2,128,1024]{3,2,1,0:T(8,128)(2,1)S(1)}, u32[]{:S(2)}, u32[]{:S(2)}) async-start(bf16[4,2,128,1024]{3,2,1,0:T(8,128)(2,1)} %select_select_fusion), calls=%async_computation.1 | async-start | bytes 4194304 | tf_op jit(solution)/shard_map/all_to_all | solution.py:70
  27.6 0.0 reduce-scatter.4.cloned.1.call-start
  27.7 8.3 %all-gather.3.cloned.1.call-done = bf16[256,2048]{1,0:T(8,128)(2,1)} async-done(((bf16[64,2048]{1,0:T(8,128)(2,1)}), bf16[256,2048]{1,0:T(8,128)(2,1)}) %all-gather.3.cloned.1.call-update) | async-done | bytes 1048592 | tf_op jit(solution)/shard_map/all_gather | solution.py:21
  36.0 1.7 convert_reduce_fusion
  37.7 27.1 %all-reduce.1 = (f32[256,1]{0,1:T(1,128)S(1)}, f32[256,1]{0,1:T(1,128)S(1)}) all-reduce(f32[256,1]{0,1:T(1,128)S(1)} %bitcast.79, f32[256,1]{0,1:T(1,128)S(1)} %bitcast.78), channel_id=1, replica_groups=mesh['grp'=2,'db'=4,'head'=2,'sub'=2] {'db'}, use_global_device_ids=true, to_apply=%region_5.6 | all-reduce | flops 512 | bytes 4096 | tf_op jit(solution)/shard_map/psum | solution.py:22
  64.8 4.8 %fusion.14 = f32[256,1024]{1,0:T(8,128)} fusion(bf16[2048,1024]{1,0:T(8,128)(2,1)} %param.9, bf16[256,2048]{1,0:T(8,128)(2,1)} %all-gather.3.cloned.1.call-done, f32[256]{0:T(256)S(1)} %bitcast.83, f32[256]{0:T(256)S(1)} %bitcast.82), kind=kOutput, calls=%fused_computation.32 | convolution fusion | flops 1075838976 | bytes 6293504 | tf_op jit(solution)/shard_map/dot_general | solution.py:28
  69.6 0.0 reduce-scatter.4.cloned.1.call-update
  69.6 0.0 all-reduce.4.cloned.1.call-start
  69.6 0.7 fusion.34
  70.3 2.6 select_reduce_fusion
  72.9 0.7 fusion.35
  73.6 2.6 compare_select_fusion.1
  76.2 0.1 compare_and_fusion
  76.3 0.0 all-to-all-done.1
  76.3 2.0 gather_fusion.1
  78.4 1.9 broadcast_select_fusion
  80.2 0.2 fusion.33
  80.4 0.3 copy.36
  80.7 0.3 copy.37
  81.0 28.6 %reduce-scatter.4.cloned.1.call-done = f32[64,1024]{1,0:T(8,128)} async-done(((f32[256,1024]{1,0:T(8,128)}), f32[64,1024]{1,0:T(8,128)}) %reduce-scatter.4.cloned.1.call-update) | async-done | bytes 262160 | tf_op jit(solution)/shard_map/reduce_scatter | solution.py:27
  109.6 1.5 fusion.6
  111.0 0.3 fusion.36
  111.3 1.0 fusion.7
  112.4 0.1 bitcast_select_fusion
  112.5 12.1 %all_gather.10 = bf16[256,1024]{1,0:T(8,128)(2,1)S(1)} all-gather(bf16[64,1024]{1,0:T(8,128)(2,1)S(1)} %bitcast_select_fusion), channel_id=1, replica_groups=mesh['grp'=2,'db'=4,'head'=2,'sub'=2] {'db'}, dimensions={0}, use_global_device_ids=true | all-gather | bytes 655360 | tf_op jit(solution)/shard_map/all_gather | solution.py:91
  124.6 4.8 %fusion.37 = f32[256,2048]{1,0:T(8,128)} fusion(bf16[256,1024]{1,0:T(8,128)(2,1)S(1)} %all_gather.10, bf16[1024,2048]{1,0:T(8,128)(2,1)} %param.10), kind=kOutput, calls=%fused_computation.107 | convolution fusion | flops 1073741824 | bytes 6815744 | tf_op jit(solution)/shard_map/dot_general | solution.py:90
  129.3 0.0 copy-start
  129.4 0.0 all-reduce.4.cloned.1.call-update
  129.4 0.0 reduce-scatter.6.cloned.1.call-start
  129.4 53.9 %all-reduce.4.cloned.1.call-done = f32[256,2048]{1,0:T(8,128)} async-done(((f32[256,2048]{1,0:T(8,128)}), f32[256,2048]{1,0:T(8,128)}) %all-reduce.4.cloned.1.call-update) | async-done | bytes 2097168 | tf_op jit(solution)/shard_map/psum | solution.py:95
  183.3 0.0 copy-done
  183.4 2.0 fusion.32
  185.4 9.7 %all-reduce = (f32[256,1]{0,1:T(1,128)S(1)}, f32[256,1]{0,1:T(1,128)S(1)}) all-reduce(f32[256,1]{0,1:T(1,128)S(1)} %bitcast.77, f32[256,1]{0,1:T(1,128)S(1)} %bitcast.76), channel_id=1, replica_groups=mesh['grp'=2,'db'=4,'head'=2,'sub'=2] {'db'}, use_global_device_ids=true, to_apply=%region_13.14 | all-reduce | flops 512 | bytes 4096 | tf_op jit(solution)/shard_map/psum | solution.py:97
  195.0 11.7 %convolution_convert_fusion = bf16[256,4096]{1,0:T(8,128)(2,1)} fusion(bf16[2048,4096]{1,0:T(8,128)(2,1)} %param.11, f32[256,2048]{1,0:T(8,128)S(1)} %get-tuple-element.15, f32[256]{0:T(256)S(1)} %bitcast.81, f32[256]{0:T(256)S(1)} %bitcast.80), kind=kOutput, calls=%fused_computation.3 | convolution fusion | flops 4297588736 | bytes 20973568 | tf_op jit(solution)/shard_map/dot_general | solution.py:106
  206.8 0.0 reduce-scatter.6.cloned.1.call-update
  206.8 0.0 all-gather.5.cloned.1.call-start
  206.8 43.2 %reduce-scatter.6.cloned.1.call-done = bf16[64,4096]{1,0:T(8,128)(2,1)} async-done(((bf16[256,4096]{1,0:T(8,128)(2,1)}), bf16[64,4096]{1,0:T(8,128)(2,1)}) %reduce-scatter.6.cloned.1.call-update) | async-done | bytes 524304 | tf_op jit(solution)/shard_map/reduce_scatter | solution.py:105
  250.0 2.2 fusion.13
  252.2 0.0 all-gather.5.cloned.1.call-update
  252.3 0.2 reduce-scatter.8.cloned.1.call-start
  252.5 45.4 %all-gather.5.cloned.1.call-done = bf16[256,4096]{1,0:T(8,128)(2,1)} async-done(((bf16[64,4096]{1,0:T(8,128)(2,1)}), bf16[256,4096]{1,0:T(8,128)(2,1)}) %all-gather.5.cloned.1.call-update) | async-done | bytes 2097168 | tf_op jit(solution)/shard_map/all_gather | solution.py:112
  297.9 11.9 %convolution_convert_fusion.1 = bf16[256,2048]{1,0:T(8,128)(2,1)} fusion(bf16[256,4096]{1,0:T(8,128)(2,1)} %all-gather.5.cloned.1.call-done, bf16[4096,2048]{1,0:T(8,128)(2,1)} %param.12), kind=kOutput, calls=%fused_computation.8 | convolution fusion | flops 4295491584 | bytes 19922944 | tf_op jit(solution)/shard_map/dot_general | solution.py:115
  309.7 0.0 reduce-scatter.8.cloned.1.call-update
  309.8 23.7 %reduce-scatter.8.cloned.1.call-done = bf16[64,2048]{1,0:T(8,128)(2,1)} async-done(((bf16[256,2048]{1,0:T(8,128)(2,1)}), bf16[64,2048]{1,0:T(8,128)(2,1)}) %reduce-scatter.8.cloned.1.call-update) | async-done | bytes 262160 | tf_op jit(solution)/shard_map/reduce_scatter | solution.py:114
  333.5 1.7 add_convert_fusion
  (13 shorter events, 0.1 us)
Async XLA Ops:
  9.3 9.7 %all-to-all-start = ((s32[4,1,1]{2,1,0:T(1,128)}), s32[4,1,1]{2,1,0:T(1,128)S(1)}, u32[]{:S(2)}, u32[]{:S(2)}) async-start(s32[4,1,1]{2,1,0:T(1,128)} %copy.29), calls=%async_computation | async-start | bytes 4096 | tf_op jit(solution)/shard_map/all_to_all | solution.py:61
  14.7 21.3 %all-gather.3.cloned.1.call-start = ((), (), s32[]{:S(2)}) async-start(), calls=%async_computation.5 | async-start | bytes 1310720 | tf_op jit(solution)/shard_map/all_gather | solution.py:21
  24.0 52.3 %all-to-all-start.1 = ((bf16[4,2,128,1024]{3,2,1,0:T(8,128)(2,1)}), bf16[4,2,128,1024]{3,2,1,0:T(8,128)(2,1)S(1)}, u32[]{:S(2)}, u32[]{:S(2)}) async-start(bf16[4,2,128,1024]{3,2,1,0:T(8,128)(2,1)} %select_select_fusion), calls=%async_computation.1 | async-start | bytes 4194304 | tf_op jit(solution)/shard_map/all_to_all | solution.py:70
  27.6 81.9 %reduce-scatter.4.cloned.1.call-start = ((), (), s32[]{:S(2)}) async-start(), calls=%async_computation.6 | async-start | bytes 1310720 | tf_op jit(solution)/shard_map/reduce_scatter | solution.py:27
  69.6 113.8 %all-reduce.4.cloned.1.call-start = ((), (), s32[]{:S(2)}) async-start(), calls=%async_computation.7 | async-start | bytes 4194304 | tf_op jit(solution)/shard_map/psum | solution.py:95
  129.3 54.0 %copy-start = (bf16[256,2048]{1,0:T(8,128)(2,1)S(1)}, bf16[256,2048]{1,0:T(8,128)(2,1)}, u32[]{:S(2)}) copy-start(bf16[256,2048]{1,0:T(8,128)(2,1)} %all-gather.3.cloned.1.call-done) | copy-start | bytes 3145732
  129.4 120.7 %reduce-scatter.6.cloned.1.call-start = ((), (), s32[]{:S(2)}) async-start(), calls=%async_computation.8 | async-start | bytes 2621440 | tf_op jit(solution)/shard_map/reduce_scatter | solution.py:105
  206.8 91.1 %all-gather.5.cloned.1.call-start = ((), (), s32[]{:S(2)}) async-start(), calls=%async_computation.9 | async-start | bytes 2621440 | tf_op jit(solution)/shard_map/all_gather | solution.py:112
  252.3 81.2 %reduce-scatter.8.cloned.1.call-start = ((), (), s32[]{:S(2)}) async-start(), calls=%async_computation.10 | async-start | bytes 1310720 | tf_op jit(solution)/shard_map/reduce_scatter | solution.py:114
Sparse Core Ops, SparseCore 0:
  17.1 18.8 all-gather.2
  69.7 39.8 reduce-scatter.3
  129.5 53.8 all-reduce.3
  206.9 43.0 reduce-scatter.5
  252.4 45.4 all-gather.4
  309.9 23.5 reduce-scatter.7
where the time goes:
time: 343 us; the launch traced here: 342 us
  waiting for transfers between devices  208 us (61%)
  blocking collectives  48.8 us (14%)
  matrix products  35.7 us (10%)
  other arithmetic  18.3 us (5%)
  between operations  13.6 us (4%)
  starting transfers between devices  9.42 us (3%)
  local copies, waits for them, and re-layouts  8.63 us (3%)
    psum x1, waiting for transfers between devices, local(): attn_full = lax.psum(attn_part, ('head', 'sub'))  53.9 us
    all_gather x1, waiting for transfers between devices, local(): gathered = lax.all_gather(activated, 'db', axis=0, tiled=True)  45.4 us
    reduce_scatter x1, waiting for transfers between devices, local(): lax.psum_scatter(jnp.dot(normed_mid, w_up, preferred_element_type=jnp.flo...  43.2 us
    reduce_scatter x1, waiting for transfers between devices, local(): lax.psum_scatter(jnp.dot(normed, w_query, preferred_element_type=jnp.floa...  28.6 us
    psum x1, blocking collectives, local(): lax.psum((jnp.sum(inputs, axis=1, keepdims=True), jnp.sum(inputs * inputs...  27.1 us
    reduce_scatter x1, waiting for transfers between devices, local(): lax.psum_scatter(jnp.dot(gathered, w_down, preferred_element_type=jnp.flo...  23.7 us
    all_gather x1, blocking collectives, local(): lax.all_gather(attended, 'db', axis=0, tiled=True)  12.1 us
    dot_general x1, matrix products, local(): jnp.dot(gathered, w_down, preferred_element_type=jnp.float32)  11.9 us
  transfers between devices with their start and end apart: 8, of which 7 were waited for; matrix products, arithmetic and copies ran while one was open for 7% of the time, Pallas kernels for 0%

commit v1 on v0

--- a/solution.py
+++ b/solution.py
@@ -1,12 +1,15 @@
 import jax
 import jax.numpy as jnp
 from jax import lax
+from jax.experimental import pallas as pl
+from jax.experimental.pallas import tpu as pltpu
 from jax.sharding import PartitionSpec as P
 
 D = 8192
 HDIM = 128
 NEIGH = 2
 NTOK = 128
+VMEM_BYTES = 63 * 1024 * 1024
 
 
 def apply_norm(values, row_sums):
@@ -123,6 +126,328 @@
     return (own_state + lowered).astype(jnp.bfloat16)
 
 
+def dot(left, right):
+    return jnp.dot(left, right, preferred_element_type=jnp.float32)
+
+
+def layer_kernel(
+    act, wq_hbm, wo_hbm, wu_hbm, wd_hbm, kv_hbm, near, place, out,
+    wq, wu, wd, kvs, xg, st_in, st_tot, nx, qp, qr, qg, ob, lse, att,
+    op, orx, state, st_mid, ng, lp, lr, ag, acc, dp, dr,
+    local_sem, wd0_sem, x_s, x_r, si_s, si_r, st_s, st_r, qp_s, qp_r, qg_s, qg_r,
+    ob_s, ob_r, ls_s, ls_r, op_s, op_r, sm_s, sm_r, ng_s, ng_r,
+    lp_s, lp_r, ag_s, ag_r, dp_s, dp_r,
+):
+    f32, bf16 = jnp.float32, jnp.bfloat16
+    me = lax.axis_index("db")
+    hs = lax.axis_index("head") * 2 + lax.axis_index("sub")
+    rows, width = act.shape
+    heads = wq.shape[1] // HDIM
+    store = kvs.shape[0]
+
+    def db_at(k):
+        return lax.rem(me + k, 4)
+
+    def hs_at(k):
+        return lax.rem(hs + k, 4)
+
+    def db_copy(src, dst, send, recv, k):
+        return pltpu.make_async_remote_copy(
+            src_ref=src, dst_ref=dst, send_sem=send, recv_sem=recv,
+            device_id={"db": db_at(k)}, device_id_type=pl.DeviceIdType.MESH,
+        )
+
+    def hs_copy(src, dst, send, recv, k):
+        peer = hs_at(k)
+        return pltpu.make_async_remote_copy(
+            src_ref=src, dst_ref=dst, send_sem=send, recv_sem=recv,
+            device_id={"head": lax.div(peer, 2), "sub": lax.rem(peer, 2)},
+            device_id_type=pl.DeviceIdType.MESH,
+        )
+
+    loads = [
+        pltpu.make_async_copy(wq_hbm, wq, local_sem.at[0]),
+        pltpu.make_async_copy(wo_hbm, wd.at[0], local_sem.at[1]),
+        pltpu.make_async_copy(kv_hbm, kvs, local_sem.at[2]),
+        pltpu.make_async_copy(wu_hbm, wu, local_sem.at[3]),
+    ]
+    for c in range(1, 4):
+        loads.append(
+            pltpu.make_async_copy(wd_hbm.at[pl.ds(c * 1024, 1024)], wd.at[c], local_sem.at[3 + c])
+        )
+    for load in loads:
+        load.start()
+
+    barrier = pltpu.get_barrier_semaphore()
+    for k in (1, 2, 3):
+        pl.semaphore_signal(
+            barrier, inc=1, device_id={"db": db_at(k)}, device_id_type=pl.DeviceIdType.MESH
+        )
+        peer = hs_at(k)
+        pl.semaphore_signal(
+            barrier, inc=1, device_id={"head": lax.div(peer, 2), "sub": lax.rem(peer, 2)},
+            device_id_type=pl.DeviceIdType.MESH,
+        )
+    pl.semaphore_wait(barrier, 6)
+
+    sends = []
+
+    def go(copy):
+        copy.start()
+        sends.append(copy)
+        return copy
+
+    def row_sums(values):
+        total = jnp.sum(values, axis=1, keepdims=True)
+        square = jnp.sum(values * values, axis=1, keepdims=True)
+        return jnp.concatenate(
+            [jnp.broadcast_to(total, (rows, 128)), jnp.broadcast_to(square, (rows, 128))], axis=1
+        )
+
+    def mean_and_scale(sums):
+        row_mean = sums[:, 0:1] / D
+        row_var = sums[:, 128:129] / D - row_mean * row_mean
+        return row_mean, lax.rsqrt(row_var + 1e-05)
+
+    xs = [go(hs_copy(act, xg.at[hs], x_s.at[k - 1], x_r.at[k - 1], k)) for k in (1, 2, 3)]
+    st_in[me] = row_sums(act[...].astype(f32))
+    copies = [go(db_copy(st_in.at[me], st_in.at[me], si_s.at[k - 1], si_r.at[k - 1], k)) for k in (1, 2, 3)]
+    xg[hs] = act[...]
+    for copy in copies:
+        copy.wait_recv()
+    st_tot[hs] = st_in[0] + st_in[1] + st_in[2] + st_in[3]
+    copies = [go(hs_copy(st_tot.at[hs], st_tot.at[hs], st_s.at[k - 1], st_r.at[k - 1], k)) for k in (1, 2, 3)]
+    for copy in copies:
+        copy.wait_recv()
+    for copy in xs:
+        copy.wait_recv()
+
+    all_mean, all_scale = mean_and_scale(st_tot[...].reshape(4 * rows, 256))
+
+    def norm_tile(t, carry):
+        cols = pl.ds(pl.multiple_of(t * 512, 512), 512)
+        values = xg[:, :, cols].reshape(4 * rows, 512).astype(f32)
+        values = (values - all_mean) * all_scale
+        nx[:, cols] = pltpu.roll(values, 4 * rows - (rows - 1), 0).astype(bf16)
+        return carry
+
+    lax.fori_loop(0, width // 512, norm_tile, 0)
+
+    loads[0].wait()
+
+    def query_tile(t, carry):
+        cols = pl.ds(pl.multiple_of(t * 512, 512), 512)
+        qp[:, :, cols] = dot(nx[...], wq[:, cols]).astype(bf16).reshape(4, rows, 512)
+        return carry
+
+    lax.fori_loop(0, wq.shape[1] // 512, query_tile, 0)
+    copies = [
+        go(db_copy(qp.at[db_at(k)], qr.at[me], qp_s.at[k - 1], qp_r.at[k - 1], k)) for k in (1, 2, 3)
+    ]
+    for copy in copies:
+        copy.wait_recv()
+    total = qp[me].astype(f32)
+    for k in (1, 2, 3):
+        total = total + qr[db_at(k)].astype(f32)
+    qg[me] = total.astype(bf16)
+    copies = [go(db_copy(qg.at[me], qg.at[me], qg_s.at[k - 1], qg_r.at[k - 1], k)) for k in (1, 2, 3)]
+    loads[2].wait()
+    for copy in copies:
+        copy.wait_recv()
+
+    def spot(a, n):
+        return place[near[a, n]]
+
+    def owner(a, n):
+        return lax.div(spot(a, n), store)
+
+    odd = jnp.where((owner(1, 0) == me) | (owner(1, 1) == me), 1, 0)
+    lane = lax.broadcasted_iota(jnp.int32, (rows, 128), 1)
+    logs = jnp.zeros((rows, 128), f32)
+    for r in range(2):
+        span = 2 * r + odd
+        which = jnp.where(owner(span, 1) == me, 1, 0)
+        slot = lax.rem(spot(span, which), store)
+        for h in range(heads):
+            cols = slice(h * HDIM, (h + 1) * HDIM)
+            scores = lax.dot_general(
+                qg[span, :, cols], kvs[slot, 0, :, cols], (((1,), (1,)), ((), ())),
+                preferred_element_type=f32,
+            ) * HDIM ** (-0.5)
+            top = jnp.max(scores, axis=1, keepdims=True)
+            raised = jnp.exp(scores - top)
+            norm = jnp.sum(raised, axis=1, keepdims=True)
+            ob[me, r, :, cols] = dot(
+                (raised / norm).astype(bf16), kvs[slot, 1, :, cols]
+            ).astype(bf16)
+            logs = jnp.where(lane == r * heads + h, top + jnp.log(norm), logs)
+    lse[me] = logs
+    copies = []
+    for k in (1, 2, 3):
+        copies.append(go(db_copy(lse.at[me], lse.at[me], ls_s.at[k - 1], ls_r.at[k - 1], k)))
+        copies.append(go(db_copy(ob.at[me], ob.at[me], ob_s.at[k - 1], ob_r.at[k - 1], k)))
+    loads[1].wait()
+    for copy in copies:
+        copy.wait_recv()
+    for a in range(4):
+        r = a // 2
+        first, second = owner(a, 0), owner(a, 1)
+        log_a, log_b = lse[first], lse[second]
+        for h in range(heads):
+            cols = slice(h * HDIM, (h + 1) * HDIM)
+            at = r * heads + h
+            gap = log_b[:, at:at + 1] - log_a[:, at:at + 1]
+            mixed = ob[first, r, :, cols].astype(f32) / (1.0 + jnp.exp(gap)) + ob[
+                second, r, :, cols
+            ].astype(f32) / (1.0 + jnp.exp(-gap))
+            att[a * rows:(a + 1) * rows, cols] = mixed.astype(bf16)
+
+    def out_tile(t, carry):
+        cols = pl.ds(pl.multiple_of(t * 512, 512), 512)
+        part = pltpu.roll(dot(att[...], wd[0, :, cols]), rows - 1, 0)
+        row_id = lax.broadcasted_iota(jnp.int32, part.shape, 0)
+        part = jnp.where(row_id < rows - 1, 0.0, part)
+        op[:, :, cols] = part.astype(bf16).reshape(4, rows, 512)
+        return carry
+
+    lax.fori_loop(0, width // 512, out_tile, 0)
+    copies = [
+        go(hs_copy(op.at[hs_at(k)], orx.at[hs], op_s.at[k - 1], op_r.at[k - 1], k)) for k in (1, 2, 3)
+    ]
+    first_down = pltpu.make_async_copy(wd_hbm.at[pl.ds(0, 1024)], wd.at[0], wd0_sem)
+    first_down.start()
+    for copy in copies:
+        copy.wait_recv()
+    total = act[...].astype(f32) + op[hs].astype(f32)
+    for k in (1, 2, 3):
+        total = total + orx[hs_at(k)].astype(f32)
+    state[...] = total
+    st_mid[me] = row_sums(total)
+    copies = [go(db_copy(st_mid.at[me], st_mid.at[me], sm_s.at[k - 1], sm_r.at[k - 1], k)) for k in (1, 2, 3)]
+    for copy in copies:
+        copy.wait_recv()
+    row_mean, row_scale = mean_and_scale(st_mid[0] + st_mid[1] + st_mid[2] + st_mid[3])
+    ng[hs] = ((state[...] - row_mean) * row_scale).astype(bf16)
+    copies = [go(hs_copy(ng.at[hs], ng.at[hs], ng_s.at[k - 1], ng_r.at[k - 1], k)) for k in (1, 2, 3)]
+    loads[3].wait()
+    for copy in copies:
+        copy.wait_recv()
+
+    def lift_copy(c, k):
+        return db_copy(
+            lp.at[c, db_at(k)], lr.at[c, me], lp_s.at[c, k - 1], lp_r.at[c, k - 1], k
+        )
+
+    def up_tile(c, carry):
+        for half in range(2):
+            cols = pl.ds(pl.multiple_of(c * 1024 + half * 512, 512), 512)
+            part = dot(ng[...].reshape(4 * rows, width), wu[:, cols])
+            lp[c, :, :, half * 512:(half + 1) * 512] = part.astype(bf16).reshape(4, rows, 512)
+        for k in (1, 2, 3):
+            lift_copy(c, k).start()
+        return carry
+
+    lax.fori_loop(0, 4, up_tile, 0)
+
+    def lifted_copy(c, k):
+        return db_copy(ag.at[c, me], ag.at[c, me], ag_s.at[c, k - 1], ag_r.at[c, k - 1], k)
+
+    def gelu_tile(c, carry):
+        for k in (1, 2, 3):
+            lift_copy(c, k).wait()
+        for half in range(2):
+            cols = slice(half * 512, (half + 1) * 512)
+            total = lp[c, me, :, cols].astype(f32)
+            for k in (1, 2, 3):
+                total = total + lr[c, db_at(k), :, cols].astype(f32)
+            ag[c, me, :, cols] = jax.nn.gelu(total, approximate=True).astype(bf16)
+        for k in (1, 2, 3):
+            lifted_copy(c, k).start()
+        return carry
+
+    lax.fori_loop(0, 4, gelu_tile, 0)
+
+    acc[...] = jnp.zeros_like(acc)
+    first_down.wait()
+    for load in loads[4:]:
+        load.wait()
+
+    def down_tile(c, carry):
+        for k in (1, 2, 3):
+            lifted_copy(c, k).wait()
+        for t in range(4):
+            cols = slice(t * 512, (t + 1) * 512)
+            acc[:, cols] += dot(ag[c].reshape(4 * rows, 1024), wd[c, :, cols])
+        return carry
+
+    lax.fori_loop(0, 4, down_tile, 0)
+    dp[...] = acc[...].astype(bf16).reshape(dp.shape)
+    copies = [
+        go(hs_copy(dp.at[hs_at(k)], dr.at[hs], dp_s.at[k - 1], dp_r.at[k - 1], k)) for k in (1, 2, 3)
+    ]
+    for copy in copies:
+        copy.wait_recv()
+    total = state[...] + dp[hs].astype(f32)
+    for k in (1, 2, 3):
+        total = total + dr[hs_at(k)].astype(f32)
+    out[...] = total.astype(bf16)
+    for copy in sends:
+        copy.wait_send()
+
+
+def fused(activations, w_query, w_out, w_up, w_down, kv_store, neighbours, block_place):
+    f32, bf16 = jnp.float32, jnp.bfloat16
+    rows, width = activations.shape
+    qw = w_query.shape[1]
+    hidden = w_up.shape[1]
+    vmem = pl.BlockSpec(memory_space=pltpu.VMEM)
+    smem = pl.BlockSpec(memory_space=pltpu.SMEM)
+    hbm = pl.BlockSpec(memory_space=pl.ANY)
+    tile = hidden // 4
+    scratch = [
+        pltpu.VMEM(w_query.shape, bf16),
+        pltpu.VMEM(w_up.shape, bf16),
+        pltpu.VMEM((4, tile, width), bf16),
+        pltpu.VMEM(kv_store.shape, bf16),
+        pltpu.VMEM((4, rows, width), bf16),
+        pltpu.VMEM((4, rows, 256), f32),
+        pltpu.VMEM((4, rows, 256), f32),
+        pltpu.VMEM((4 * rows, width), bf16),
+        pltpu.VMEM((4, rows, qw), bf16),
+        pltpu.VMEM((4, rows, qw), bf16),
+        pltpu.VMEM((4, rows, qw), bf16),
+        pltpu.VMEM((4, 2, rows, qw), bf16),
+        pltpu.VMEM((4, rows, 128), f32),
+        pltpu.VMEM((4 * rows, qw), bf16),
+        pltpu.VMEM((4, rows, width), bf16),
+        pltpu.VMEM((4, rows, width), bf16),
+        pltpu.VMEM((rows, width), f32),
+        pltpu.VMEM((4, rows, 256), f32),
+        pltpu.VMEM((4, rows, width), bf16),
+        pltpu.VMEM((4, 4, rows, tile), bf16),
+        pltpu.VMEM((4, 4, rows, tile), bf16),
+        pltpu.VMEM((4, 4, rows, tile), bf16),
+        pltpu.VMEM((4 * rows, width), f32),
+        pltpu.VMEM((4, rows, width), bf16),
+        pltpu.VMEM((4, rows, width), bf16),
+        pltpu.SemaphoreType.DMA((7,)),
+        pltpu.SemaphoreType.DMA,
+    ]
+    scratch += [pltpu.SemaphoreType.DMA((3,)) for _ in range(20)]
+    scratch += [pltpu.SemaphoreType.DMA((4, 3)) for _ in range(4)]
+    scratch += [pltpu.SemaphoreType.DMA((3,)) for _ in range(2)]
+    return pl.pallas_call(
+        layer_kernel,
+        out_shape=jax.ShapeDtypeStruct((rows, width), bf16),
+        in_specs=[vmem, hbm, hbm, hbm, hbm, hbm, smem, smem],
+        out_specs=vmem,
+        scratch_shapes=scratch,
+        compiler_params=pltpu.CompilerParams(
+            collective_id=0, has_side_effects=True, vmem_limit_bytes=VMEM_BYTES
+        ),
+    )(activations, w_query, w_out, w_up, w_down, kv_store, neighbours, block_place)
+
+
 def solution(mesh):
     in_specs = (
         P(("grp", "head", "sub"), "db"),
@@ -135,4 +460,6 @@
         P("grp"),
     )
     out_specs = P(("grp", "head", "sub"), "db")
-    return jax.shard_map(local, mesh=mesh, in_specs=in_specs, out_specs=out_specs, check_vma=False)
+    sizes = mesh.shape
+    body = fused if (sizes["db"], sizes["head"], sizes["sub"]) == (4, 2, 2) else local
+    return jax.shard_map(body, mesh=mesh, in_specs=in_specs, out_specs=out_specs, check_vma=False)

time: 343 us -> 216 us (0.63)
  Pallas kernels: 0 us -> 212 us
  waiting for transfers between devices: 208 us -> 0 us
  blocking collectives: 48.8 us -> 0 us
  matrix products: 35.7 us -> 0 us
  other arithmetic: 18.3 us -> 0 us
  between operations: 13.6 us -> 0.01 us
  starting transfers between devices: 9.42 us -> 0 us
  local copies, waits for them, and re-layouts: 8.63 us -> 3.01 us
    pallas_call x0 -> x1, Pallas kernels: none -> 212 us  [fused(): pl.pallas_call(layer_kernel, out_shape=jax.ShapeDtypeStruct((rows, width)...]
    reduce_scatter x3 -> x0, waiting for transfers between devices: 95.5 us -> none  [the longest x1 43.2 us: local(): lax.psum_scatter(jnp.dot(normed_mid, w_up, preferred_element_type=jnp.flo...]
    psum x1 -> x0, waiting for transfers between devices: 53.9 us -> none  [local(): attn_full = lax.psum(attn_part, ('head', 'sub'))]
    all_gather x2 -> x0, waiting for transfers between devices: 53.7 us -> none  [the longest x1 45.4 us: local(): gathered = lax.all_gather(activated, 'db', axis=0, tiled=True)]
    psum x2 -> x0, blocking collectives: 36.7 us -> none  [the longest x1 27.1 us: local(): lax.psum((jnp.sum(inputs, axis=1, keepdims=True), jnp.sum(inputs * inputs...]
    dot_general x6 -> x0, matrix products: 35.7 us -> none  [the longest x1 11.9 us: local(): jnp.dot(gathered, w_down, preferred_element_type=jnp.float32)]
    all_gather x1 -> x0, blocking collectives: 12.1 us -> none  [local(): lax.all_gather(attended, 'db', axis=0, tiled=True)]
    all_to_all x2 -> x0, starting transfers between devices: 9.03 us -> none  [the longest x1 5.42 us: local(): lax.all_to_all(request_out, 'db', split_axis=0, concat_axis=0, tiled=True)]
  transfers between devices with their start and end apart: 8 -> 0, of which waited for: 7 -> 0; matrix products, arithmetic and copies ran while one was open for 7% -> 0% of each run, Pallas kernels for 0% -> 0%
where the time goes in v1:
time: 216 us; the launch traced here: 215 us
  Pallas kernels  212 us (98%)
  local copies, waits for them, and re-layouts  3.01 us (1%)
    pallas_call x1, Pallas kernels, fused(): pl.pallas_call(layer_kernel, out_shape=jax.ShapeDtypeStruct((rows, width)...  212 us

profile of v1, /device:TPU:1, one launch (start us, length us, event | category | flops | bytes accessed | tf_op | source)
XLA Modules:
  0.0 215.0 jit_solution(16792751117120538066)
XLA Ops:
  0.0 1.3 copy.9.near
  1.3 212.0 %shard_map.82 = bf16[64,2048]{1,0:T(8,128)(2,1)} custom-call(bf16[64,2048]{1,0:T(8,128)(2,1)} %act.1, bf16[2048,1024]{1,0:T(8,128)(2,1)} %wq_hbm.1, bf16[1024,2048]{1,0:T(8,128)(2,1)} %wo_hbm.1, bf16[2048,4096]{1,0:T(8,128)(2,1)} %wu_hbm.1, bf16[4096,2048]{1,0:T(8,128)(2,1)} %wd_hbm.1, bf16[8,2,128,1024]{3,2,1,0:T(8,128)(2,1)} %kv_hbm.1, s32[4,2]{1,0:T(4,128)} %copy.9.near, ...), custom_call_target="tpu_custom_call" | custom-call | tf_op jit(solution)/shard_map/pallas_call | solution.py:439
  213.3 1.7 copy.11

commit v2 on v1

--- a/solution.py
+++ b/solution.py
@@ -9,6 +9,7 @@
 HDIM = 128
 NEIGH = 2
 NTOK = 128
+PIECES = 16
 VMEM_BYTES = 63 * 1024 * 1024
 
 
@@ -135,8 +136,8 @@
     wq, wu, wd, kvs, xg, st_in, st_tot, nx, qp, qr, qg, ob, lse, att,
     op, orx, state, st_mid, ng, lp, lr, ag, acc, dp, dr,
     local_sem, wd0_sem, x_s, x_r, si_s, si_r, st_s, st_r, qp_s, qp_r, qg_s, qg_r,
-    ob_s, ob_r, ls_s, ls_r, op_s, op_r, sm_s, sm_r, ng_s, ng_r,
-    lp_s, lp_r, ag_s, ag_r, dp_s, dp_r,
+    ob_s, ob_r, ls_s, ls_r, op_s, op_r, sm_s, sm_r, ng_s, ng_r, dp_s, dp_r,
+    lp_s, lp_r, ag_s, ag_r,
 ):
     f32, bf16 = jnp.float32, jnp.bfloat16
     me = lax.axis_index("db")
@@ -167,13 +168,13 @@
 
     loads = [
         pltpu.make_async_copy(wq_hbm, wq, local_sem.at[0]),
-        pltpu.make_async_copy(wo_hbm, wd.at[0], local_sem.at[1]),
+        pltpu.make_async_copy(wo_hbm, wd.at[pl.ds(0, 1024)], local_sem.at[1]),
         pltpu.make_async_copy(kv_hbm, kvs, local_sem.at[2]),
         pltpu.make_async_copy(wu_hbm, wu, local_sem.at[3]),
     ]
     for c in range(1, 4):
         loads.append(
-            pltpu.make_async_copy(wd_hbm.at[pl.ds(c * 1024, 1024)], wd.at[c], local_sem.at[3 + c])
+            pltpu.make_async_copy(wd_hbm.at[pl.ds(c * 1024, 1024)], wd.at[pl.ds(c * 1024, 1024)], local_sem.at[3 + c])
         )
     for load in loads:
         load.start()
@@ -196,6 +197,48 @@
         copy.start()
         sends.append(copy)
         return copy
+
+    head, sub = lax.axis_index("head"), lax.axis_index("sub")
+    across = (1 - head) * 2 + sub
+    beside = head * 2 + 1 - sub
+    far = (1 - head) * 2 + 1 - sub
+
+    def send_across(src, dst, send, recv):
+        return pltpu.make_async_remote_copy(
+            src_ref=src, dst_ref=dst, send_sem=send, recv_sem=recv,
+            device_id={"head": 1 - head}, device_id_type=pl.DeviceIdType.MESH,
+        )
+
+    def send_beside(src, dst, send, recv):
+        return pltpu.make_async_remote_copy(
+            src_ref=src, dst_ref=dst, send_sem=send, recv_sem=recv,
+            device_id={"sub": 1 - sub}, device_id_type=pl.DeviceIdType.MESH,
+        )
+
+    def spread(own, buffer, send, recv):
+        first = go(send_across(own, buffer.at[hs], send.at[0], recv.at[0]))
+        second = go(send_beside(own, buffer.at[hs], send.at[1], recv.at[1]))
+
+        def finish():
+            first.wait_recv()
+            third = go(
+                send_beside(buffer.at[across], buffer.at[across], send.at[2], recv.at[2])
+            )
+            second.wait_recv()
+            third.wait_recv()
+
+        return finish
+
+    def reduce_to_owner(parts, landing, send, recv):
+        first = go(send_beside(parts.at[far], landing.at[0], send.at[0], recv.at[0]))
+        second = go(send_beside(parts.at[beside], landing.at[1], send.at[1], recv.at[1]))
+        first.wait_recv()
+        parts[across] = (parts[across].astype(f32) + landing[0].astype(f32)).astype(bf16)
+        third = go(send_across(parts.at[across], landing.at[2], send.at[2], recv.at[2]))
+        second.wait_recv()
+        total = parts[hs].astype(f32) + landing[1].astype(f32)
+        third.wait_recv()
+        return total + landing[2].astype(f32)
 
     def row_sums(values):
         total = jnp.sum(values, axis=1, keepdims=True)
@@ -209,7 +252,7 @@
         row_var = sums[:, 128:129] / D - row_mean * row_mean
         return row_mean, lax.rsqrt(row_var + 1e-05)
 
-    xs = [go(hs_copy(act, xg.at[hs], x_s.at[k - 1], x_r.at[k - 1], k)) for k in (1, 2, 3)]
+    finish = spread(act, xg, x_s, x_r)
     st_in[me] = row_sums(act[...].astype(f32))
     copies = [go(db_copy(st_in.at[me], st_in.at[me], si_s.at[k - 1], si_r.at[k - 1], k)) for k in (1, 2, 3)]
     xg[hs] = act[...]
@@ -219,8 +262,7 @@
     copies = [go(hs_copy(st_tot.at[hs], st_tot.at[hs], st_s.at[k - 1], st_r.at[k - 1], k)) for k in (1, 2, 3)]
     for copy in copies:
         copy.wait_recv()
-    for copy in xs:
-        copy.wait_recv()
+    finish()
 
     all_mean, all_scale = mean_and_scale(st_tot[...].reshape(4 * rows, 256))
 
@@ -304,23 +346,18 @@
 
     def out_tile(t, carry):
         cols = pl.ds(pl.multiple_of(t * 512, 512), 512)
-        part = pltpu.roll(dot(att[...], wd[0, :, cols]), rows - 1, 0)
+        part = pltpu.roll(dot(att[...], wd[pl.ds(0, 1024), cols]), rows - 1, 0)
         row_id = lax.broadcasted_iota(jnp.int32, part.shape, 0)
         part = jnp.where(row_id < rows - 1, 0.0, part)
         op[:, :, cols] = part.astype(bf16).reshape(4, rows, 512)
         return carry
 
     lax.fori_loop(0, width // 512, out_tile, 0)
-    copies = [
-        go(hs_copy(op.at[hs_at(k)], orx.at[hs], op_s.at[k - 1], op_r.at[k - 1], k)) for k in (1, 2, 3)
-    ]
-    first_down = pltpu.make_async_copy(wd_hbm.at[pl.ds(0, 1024)], wd.at[0], wd0_sem)
+    total = act[...].astype(f32) + reduce_to_owner(op, orx, op_s, op_r)
+    first_down = pltpu.make_async_copy(
+        wd_hbm.at[pl.ds(0, 1024)], wd.at[pl.ds(0, 1024)], wd0_sem
+    )
     first_down.start()
-    for copy in copies:
-        copy.wait_recv()
-    total = act[...].astype(f32) + op[hs].astype(f32)
-    for k in (1, 2, 3):
-        total = total + orx[hs_at(k)].astype(f32)
     state[...] = total
     st_mid[me] = row_sums(total)
     copies = [go(db_copy(st_mid.at[me], st_mid.at[me], sm_s.at[k - 1], sm_r.at[k - 1], k)) for k in (1, 2, 3)]
@@ -328,69 +365,106 @@
         copy.wait_recv()
     row_mean, row_scale = mean_and_scale(st_mid[0] + st_mid[1] + st_mid[2] + st_mid[3])
     ng[hs] = ((state[...] - row_mean) * row_scale).astype(bf16)
-    copies = [go(hs_copy(ng.at[hs], ng.at[hs], ng_s.at[k - 1], ng_r.at[k - 1], k)) for k in (1, 2, 3)]
+    finish = spread(ng.at[hs], ng, ng_s, ng_r)
     loads[3].wait()
-    for copy in copies:
-        copy.wait_recv()
-
-    def lift_copy(c, k):
-        return db_copy(
-            lp.at[c, db_at(k)], lr.at[c, me], lp_s.at[c, k - 1], lp_r.at[c, k - 1], k
-        )
-
-    def up_tile(c, carry):
-        for half in range(2):
-            cols = pl.ds(pl.multiple_of(c * 1024 + half * 512, 512), 512)
-            part = dot(ng[...].reshape(4 * rows, width), wu[:, cols])
-            lp[c, :, :, half * 512:(half + 1) * 512] = part.astype(bf16).reshape(4, rows, 512)
-        for k in (1, 2, 3):
-            lift_copy(c, k).start()
-        return carry
-
-    lax.fori_loop(0, 4, up_tile, 0)
-
-    def lifted_copy(c, k):
-        return db_copy(ag.at[c, me], ag.at[c, me], ag_s.at[c, k - 1], ag_r.at[c, k - 1], k)
-
-    def gelu_tile(c, carry):
-        for k in (1, 2, 3):
-            lift_copy(c, k).wait()
-        for half in range(2):
-            cols = slice(half * 512, (half + 1) * 512)
-            total = lp[c, me, :, cols].astype(f32)
-            for k in (1, 2, 3):
-                total = total + lr[c, db_at(k), :, cols].astype(f32)
-            ag[c, me, :, cols] = jax.nn.gelu(total, approximate=True).astype(bf16)
-        for k in (1, 2, 3):
-            lifted_copy(c, k).start()
-        return carry
-
-    lax.fori_loop(0, 4, gelu_tile, 0)
-
-    acc[...] = jnp.zeros_like(acc)
+
+    finish()
+
+    pieces, wide = lp.shape[1], lp.shape[3]
+    half = 2 * rows
     first_down.wait()
     for load in loads[4:]:
         load.wait()
-
-    def down_tile(c, carry):
-        for k in (1, 2, 3):
-            lifted_copy(c, k).wait()
-        for t in range(4):
-            cols = slice(t * 512, (t + 1) * 512)
-            acc[:, cols] += dot(ag[c].reshape(4 * rows, 1024), wd[c, :, cols])
+    acc[...] = jnp.zeros_like(acc)
+    lines = ((me, lax.rem(me + 1, 4), lax.rem(me + 3, 4)), (3 - me, lax.rem(me + 3, 4), lax.rem(me + 1, 4)))
+
+    def along(src, dst, send, recv, peer):
+        return pltpu.make_async_remote_copy(
+            src_ref=src, dst_ref=dst, send_sem=send, recv_sem=recv,
+            device_id={"db": peer}, device_id_type=pl.DeviceIdType.MESH,
+        )
+
+    def sum_copy(way, c, src):
+        return along(
+            src.at[way, c], lr.at[way, c], lp_s.at[way, c], lp_r.at[way, c], lines[way][1]
+        )
+
+    def back_copy(way, c):
+        return along(
+            ag.at[way, c], ag.at[way, c], ag_s.at[way, c], ag_r.at[way, c], lines[way][2]
+        )
+
+    def step(t, carry):
+        @pl.when(t < pieces)
+        def _():
+            cols = pl.ds(pl.multiple_of(t * wide, wide), wide)
+            part = dot(ng[...].reshape(4 * rows, width), wu[:, cols])
+            lp[:, t] = part.astype(bf16).reshape(2, half, wide)
+            for way in range(2):
+
+                @pl.when(lines[way][0] == 0)
+                def _():
+                    sum_copy(way, t, lp).start()
+
+        for way in range(2):
+            spot_on = lines[way][0]
+            c = t - (2 * spot_on - 1)
+
+            @pl.when((spot_on > 0) & (c >= 0) & (c < pieces))
+            def _():
+                sum_copy(way, c, lr).wait_recv()
+                total = lr[way, c].astype(f32) + lp[way, c].astype(f32)
+
+                @pl.when(spot_on < 3)
+                def _():
+                    lr[way, c] = total.astype(bf16)
+                    sum_copy(way, c, lr).start()
+
+                @pl.when(spot_on == 3)
+                def _():
+                    ag[way, c] = jax.nn.gelu(total, approximate=True).astype(bf16)
+                    back_copy(way, c).start()
+
+        for way in range(2):
+            spot_on = lines[way][0]
+            c = t - 11 + 2 * spot_on
+
+            @pl.when((c >= 0) & (c < pieces))
+            def _():
+                @pl.when(spot_on < 3)
+                def _():
+                    back_copy(way, c).wait_recv()
+
+                    @pl.when(spot_on > 0)
+                    def _():
+                        back_copy(way, c).start()
+
+                deep = pl.ds(pl.multiple_of(c * wide, wide), wide)
+                for n in range(width // 512):
+                    cols = slice(n * 512, (n + 1) * 512)
+                    acc[way * half:(way + 1) * half, cols] += dot(ag[way, c], wd[deep, cols])
+
         return carry
 
-    lax.fori_loop(0, 4, down_tile, 0)
+    lax.fori_loop(0, pieces + 11, step, 0)
     dp[...] = acc[...].astype(bf16).reshape(dp.shape)
-    copies = [
-        go(hs_copy(dp.at[hs_at(k)], dr.at[hs], dp_s.at[k - 1], dp_r.at[k - 1], k)) for k in (1, 2, 3)
-    ]
-    for copy in copies:
-        copy.wait_recv()
-    total = state[...] + dp[hs].astype(f32)
-    for k in (1, 2, 3):
-        total = total + dr[hs_at(k)].astype(f32)
-    out[...] = total.astype(bf16)
+    total = reduce_to_owner(dp, dr, dp_s, dp_r)
+    out[...] = (state[...] + total).astype(bf16)
+
+    def drain(c, carry):
+        for way in range(2):
+
+            @pl.when(lines[way][0] < 3)
+            def _():
+                sum_copy(way, c, lr).wait_send()
+
+            @pl.when(lines[way][0] > 0)
+            def _():
+                back_copy(way, c).wait_send()
+
+        return carry
+
+    lax.fori_loop(0, pieces, drain, 0)
     for copy in sends:
         copy.wait_send()
 
@@ -403,11 +477,11 @@
     vmem = pl.BlockSpec(memory_space=pltpu.VMEM)
     smem = pl.BlockSpec(memory_space=pltpu.SMEM)
     hbm = pl.BlockSpec(memory_space=pl.ANY)
-    tile = hidden // 4
+    wide = hidden // PIECES
     scratch = [
         pltpu.VMEM(w_query.shape, bf16),
         pltpu.VMEM(w_up.shape, bf16),
-        pltpu.VMEM((4, tile, width), bf16),
+        pltpu.VMEM((hidden, width), bf16),
         pltpu.VMEM(kv_store.shape, bf16),
         pltpu.VMEM((4, rows, width), bf16),
         pltpu.VMEM((4, rows, 256), f32),
@@ -420,22 +494,21 @@
         pltpu.VMEM((4, rows, 128), f32),
         pltpu.VMEM((4 * rows, qw), bf16),
         pltpu.VMEM((4, rows, width), bf16),
-        pltpu.VMEM((4, rows, width), bf16),
+        pltpu.VMEM((3, rows, width), bf16),
         pltpu.VMEM((rows, width), f32),
         pltpu.VMEM((4, rows, 256), f32),
         pltpu.VMEM((4, rows, width), bf16),
-        pltpu.VMEM((4, 4, rows, tile), bf16),
-        pltpu.VMEM((4, 4, rows, tile), bf16),
-        pltpu.VMEM((4, 4, rows, tile), bf16),
+        pltpu.VMEM((2, PIECES, 2 * rows, wide), bf16),
+        pltpu.VMEM((2, PIECES, 2 * rows, wide), bf16),
+        pltpu.VMEM((2, PIECES, 2 * rows, wide), bf16),
         pltpu.VMEM((4 * rows, width), f32),
         pltpu.VMEM((4, rows, width), bf16),
-        pltpu.VMEM((4, rows, width), bf16),
+        pltpu.VMEM((3, rows, width), bf16),
         pltpu.SemaphoreType.DMA((7,)),
         pltpu.SemaphoreType.DMA,
     ]
-    scratch += [pltpu.SemaphoreType.DMA((3,)) for _ in range(20)]
-    scratch += [pltpu.SemaphoreType.DMA((4, 3)) for _ in range(4)]
-    scratch += [pltpu.SemaphoreType.DMA((3,)) for _ in range(2)]
+    scratch += [pltpu.SemaphoreType.DMA((3,)) for _ in range(22)]
+    scratch += [pltpu.SemaphoreType.DMA((2, PIECES)) for _ in range(4)]
     return pl.pallas_call(
         layer_kernel,
         out_shape=jax.ShapeDtypeStruct((rows, width), bf16),

time: 216 us -> 173 us (0.80)
  Pallas kernels: 212 us -> 170 us
    pallas_call x1, Pallas kernels: 212 us -> 170 us  [fused(): pl.pallas_call(layer_kernel, out_shape=jax.ShapeDtypeStruct((rows, width)...]
where the time goes in v2:
time: 173 us
  Pallas kernels  170 us (98%)
  local copies, waits for them, and re-layouts  3.01 us (2%)
    pallas_call x1, Pallas kernels, fused(): pl.pallas_call(layer_kernel, out_shape=jax.ShapeDtypeStruct((rows, width)...  170 us

profile of v2, /device:TPU:1, one launch (start us, length us, event | category | flops | bytes accessed | tf_op | source)
XLA Modules:
  0.0 173.2 jit_solution(13892354642774348849)
XLA Ops:
  0.0 1.3 copy.9.near
  1.3 170.2 %shard_map.82 = bf16[64,2048]{1,0:T(8,128)(2,1)} custom-call(bf16[64,2048]{1,0:T(8,128)(2,1)} %act.1, bf16[2048,1024]{1,0:T(8,128)(2,1)} %wq_hbm.1, bf16[1024,2048]{1,0:T(8,128)(2,1)} %wo_hbm.1, bf16[2048,4096]{1,0:T(8,128)(2,1)} %wu_hbm.1, bf16[4096,2048]{1,0:T(8,128)(2,1)} %wd_hbm.1, bf16[8,2,128,1024]{3,2,1,0:T(8,128)(2,1)} %kv_hbm.1, s32[4,2]{1,0:T(4,128)} %copy.9.near, ...), custom_call_target="tpu_custom_call" | custom-call | tf_op jit(solution)/shard_map/pallas_call | solution.py:512
  171.5 1.7 copy.11

commit v3 on v2

--- a/solution.py
+++ b/solution.py
@@ -427,7 +427,7 @@
 
         for way in range(2):
             spot_on = lines[way][0]
-            c = t - 11 + 2 * spot_on
+            c = t - 14 + 3 * spot_on
 
             @pl.when((c >= 0) & (c < pieces))
             def _():
@@ -439,14 +439,17 @@
                     def _():
                         back_copy(way, c).start()
 
-                deep = pl.ds(pl.multiple_of(c * wide, wide), wide)
-                for n in range(width // 512):
-                    cols = slice(n * 512, (n + 1) * 512)
-                    acc[way * half:(way + 1) * half, cols] += dot(ag[way, c], wd[deep, cols])
+                @pl.when(lax.rem(c, 2) == 1)
+                def _():
+                    deep = pl.ds(pl.multiple_of((c - 1) * wide, 2 * wide), 2 * wide)
+                    left = jnp.concatenate([ag[way, c - 1], ag[way, c]], axis=1)
+                    for n in range(width // 512):
+                        cols = slice(n * 512, (n + 1) * 512)
+                        acc[way * half:(way + 1) * half, cols] += dot(left, wd[deep, cols])
 
         return carry
 
-    lax.fori_loop(0, pieces + 11, step, 0)
+    lax.fori_loop(0, pieces + 14, step, 0)
     dp[...] = acc[...].astype(bf16).reshape(dp.shape)
     total = reduce_to_owner(dp, dr, dp_s, dp_r)
     out[...] = (state[...] + total).astype(bf16)

time: 173 us -> 176 us (1.017)
  Pallas kernels: 170 us -> 173 us
    pallas_call x1, Pallas kernels: 170 us -> 173 us  [fused(): pl.pallas_call(layer_kernel, out_shape=jax.ShapeDtypeStruct((rows, width)...]
where the time goes in v3:
time: 176 us
  Pallas kernels  173 us (98%)
  local copies, waits for them, and re-layouts  3.01 us (2%)
    pallas_call x1, Pallas kernels, fused(): pl.pallas_call(layer_kernel, out_shape=jax.ShapeDtypeStruct((rows, width)...  173 us

profile of v3, /device:TPU:1, one launch (start us, length us, event | category | flops | bytes accessed | tf_op | source)
XLA Modules:
  0.0 175.6 jit_solution(10758695084495888064)
XLA Ops:
  0.0 1.3 copy.9.near
  1.3 172.6 %shard_map.82 = bf16[64,2048]{1,0:T(8,128)(2,1)} custom-call(bf16[64,2048]{1,0:T(8,128)(2,1)} %act.1, bf16[2048,1024]{1,0:T(8,128)(2,1)} %wq_hbm.1, bf16[1024,2048]{1,0:T(8,128)(2,1)} %wo_hbm.1, bf16[2048,4096]{1,0:T(8,128)(2,1)} %wu_hbm.1, bf16[4096,2048]{1,0:T(8,128)(2,1)} %wd_hbm.1, bf16[8,2,128,1024]{3,2,1,0:T(8,128)(2,1)} %kv_hbm.1, s32[4,2]{1,0:T(4,128)} %copy.9.near, ...), custom_call_target="tpu_custom_call" | custom-call | tf_op jit(solution)/shard_map/pallas_call | solution.py:515
  173.9 1.7 copy.11
